TPU v7x, 32 devices: a whole 2x2x4 slice. The times are simulated.
32 devices in a mesh: grp: 2 (over x), chan: 16 (over z, y, core).
Axes of the slice: x: 2, y: 2, z: 4, core: 2. Of those that a mesh axis runs over, the one named last changes fastest.
Arguments:
- voltages: int32 [512, 2, 2, 32, 1024], P(('grp', 'chan')), parts along dimension 0, may hold values from -127 to 127
- scales: int32 [512, 1024], P(('grp', 'chan')), parts along dimension 0, may hold values from 1 to 8
- feed_positions: float32 [3, 1024], replicated, may hold values from -8 to 8
- beam_directions: float32 [3, 128], replicated, may hold values from -1 to 1
- dm_trials: int32 [256], replicated, may hold values from 0 to 255, each once
Outputs:
- dedispersed: float32 [256, 32, 256], P(None, ('grp', 'chan')), parts along dimension 1
There are 2 independent parts, one for each index of `grp`. A program takes and returns all parts, laid end to end along the dimension named above; an argument that names none is the same for every part. Nothing has to cross between parts.
Inputs may be any that keep to these rules, and one draw needn't show every extreme that they name: dm_trials holds each number of 0 to 255 once.
All inputs are finite; a program needn't handle non-finite values.
Results may differ from a plain program's by a relative error of at most 0.0046.
Values may be sent and summed in bfloat16 or wider, within the bound.
No kernel may reach another device: no remote copies, remote signals or barrier semaphores. Data moves between devices by JAX's collectives and lax.ppermute only.
A program may use at most 320 MiB of HBM per device.

v0:
```python
import math
import jax
import jax.numpy as jnp
from jax import lax
from jax.sharding import PartitionSpec as P

MAXD = 15
TWO_PI = 6.283185307179586
POWER_SCALE = 1.0 / 67108864.0


def passed_along(value, axis, steps):
    count = lax.axis_size(axis)
    leading, last = (max(0, -steps), min(count, count - steps))
    return lax.ppermute(value, axis, [(source, source + steps) for source in range(leading, last)])


def geometry_delay(feed_positions, beam_directions):
    total = feed_positions[0][:, None] * beam_directions[0][None, :]
    total = total + feed_positions[1][:, None] * beam_directions[1][None, :]
    return total + feed_positions[2][:, None] * beam_directions[2][None, :]


def channel_flat(volt_chan, scale_chan, cosine, sine):
    scale_col = scale_chan.astype(jnp.float32)[:, None]
    weight_pair = jnp.concatenate([scale_col * cosine, scale_col * sine], axis=1).astype(
        jnp.bfloat16
    )
    row_block = volt_chan.astype(jnp.bfloat16).reshape(-1, volt_chan.shape[-1])
    product = jnp.dot(row_block, weight_pair, preferred_element_type=jnp.float32)
    beam_count = cosine.shape[1]
    product = product.reshape(2, 2, volt_chan.shape[2], 2, beam_count)
    real_part = product[0, :, :, 0] - product[1, :, :, 1]
    imag_part = product[0, :, :, 1] + product[1, :, :, 0]
    detected = (
        real_part[0] * real_part[0]
        + imag_part[0] * imag_part[0]
        + (real_part[1] * real_part[1] + imag_part[1] * imag_part[1])
    )
    detected = detected * POWER_SCALE
    return (detected - jnp.mean(detected, axis=0, keepdims=True)).astype(jnp.bfloat16)


def delay_table(dm_trials, chan_total, trial_count):
    chan_ids = jnp.arange(chan_total, dtype=jnp.int32)
    upper = jnp.int32(chan_total) + chan_ids
    sweeps = jnp.int32(256 * chan_total * chan_total) // (upper * upper) - jnp.int32(64)
    return (
        dm_trials[:, None] * sweeps[None, :] * jnp.int32(MAXD + 1) // jnp.int32(trial_count * 192)
    )


def dedisperse(extended, onehots, time_steps, scaling):
    chan_total = extended.shape[0]
    beam_items = extended.shape[2]
    accumulate = jnp.zeros((onehots[0].shape[0], time_steps * beam_items), jnp.float32)
    for shift_step in range(MAXD + 1):
        segment = extended[:, shift_step : shift_step + time_steps, :].reshape(
            chan_total, time_steps * beam_items
        )
        accumulate = accumulate + jnp.dot(
            onehots[shift_step], segment, preferred_element_type=jnp.float32
        )
    return (accumulate * scaling).reshape(onehots[0].shape[0], time_steps, beam_items)


def local(voltages, scales, feed_positions, beam_directions, dm_trials):
    chan_local = voltages.shape[0]
    window = voltages.shape[3]
    groups = lax.axis_size("chan")
    half_groups = groups // 2
    chan_total = groups * chan_local
    beam_count = beam_directions.shape[1]
    block_beams = beam_count // half_groups
    time_steps = window // 2
    trial_count = dm_trials.shape[0]
    scaling = 1.0 / math.sqrt(chan_total)
    geometry = geometry_delay(feed_positions, beam_directions)
    first_chan = lax.axis_index("chan") * chan_local
    frequency = first_chan.astype(jnp.float32) / chan_total + 1.0
    phase = TWO_PI * frequency * geometry
    cosine = jnp.cos(phase)
    sine = jnp.sin(phase)
    flat = lax.map(lambda items: channel_flat(items[0], items[1], cosine, sine), (voltages, scales))
    delays = delay_table(dm_trials, chan_total, trial_count)
    onehots = [(delays == shift_step).astype(jnp.bfloat16) for shift_step in range(MAXD + 1)]
    outgoing = flat.reshape(chan_local, 2, time_steps, half_groups, block_beams)
    outgoing = outgoing.transpose(1, 3, 0, 2, 4).reshape(
        groups, chan_local, time_steps, block_beams
    )
    arrived = lax.all_to_all(outgoing, "chan", split_axis=0, concat_axis=0, tiled=True)
    arrived_block = arrived.reshape(chan_total, time_steps, arrived.shape[3])
    tail_rows = passed_along(arrived_block[:, :MAXD, :], "chan", -half_groups)
    extended = jnp.concatenate([arrived_block, tail_rows], axis=1)
    result = dedisperse(extended, onehots, time_steps, scaling)
    return result.reshape(trial_count, 1, time_steps * block_beams)


def solution(mesh):
    return jax.shard_map(
        local,
        mesh=mesh,
        in_specs=(
            P(("grp", "chan"), None, None, None, None),
            P(("grp", "chan"), None),
            P(),
            P(),
            P(),
        ),
        out_specs=P(None, ("grp", "chan"), None),
        check_vma=False,
    )
```

profile of v0, /device:TPU:0, one launch (start us, length us, event | category | flops | bytes accessed | tf_op | source)
XLA Modules:
  0.0 111.3 jit_solution(13977786807538412760)
XLA Ops:
  1.7 71.5 %while.12 = (s32[]{:T(128)}, bf16[16,32,128]{2,1,0:T(8,128)(2,1)S(1)}, s32[16,2,2,32,1024]{4,3,2,1,0:T(8,128)}, s32[16,1024]{1,0:T(8,128)}, f32[128]{0:T(128)S(1...) while((s32[]{:T(128)}, ...), condition=%wide.region_2.3_spmd.clone.clone, body=%wide.region_0.2_spmd.clone.clone.sunk | while | flops 69661696 | bytes 3083917 | solution.py:84
  2.4 2.2 %fusion.189 = (bf16[1024,128]{0,1:T(8,128)(2,1)S(1)}, bf16[1024,128]{0,1:T(8,128)(2,1)S(1)}) fusion(f32[128]{0:T(128)S(1)} %get-tuple-element.290, f32[1024]{0:T(1024)S(1)} %get-tuple-element.291, f32[128]{0:T(128)S(1)} %get-tuple-element.288, f32[1024]{0:T(1024)S(1)} %get-tuple-element.289, f32[128]{0:T(128)S(1)} %get-tuple-element.286, ...), kind=kLoop, calls=%fused_computation.6.clone.1 | loop fusion | flops 1310720 | bytes 542212 | tf_op jit(solution)/shard_map/convert
  4.7 1.4 %fusion.190 = f32[2,2,32,2,128]{4,2,3,1,0:T(8,128)S(1)} fusion(bf16[2,128,1024,1,1]{2,1,0,4,3:T(8,128)(2,1)S(1)} %bitcast.78, s32[16,2,2,32,1024]{4,3,2,1,0:T(8,128)} %get-tuple-element.284, s32[]{:T(128)S(6)} %copy.19), kind=kOutput, calls=%fused_computation.10.clone.1 | convolution fusion | flops 67239936 | bytes 1179652 | tf_op jit(solution)/shard_map/while/body/eval_jaxpr/dot_general | solution.py:30
  6.9 2.2 %fusion.189 = (bf16[1024,128]{0,1:T(8,128)(2,1)S(1)}, bf16[1024,128]{0,1:T(8,128)(2,1)S(1)}) fusion(f32[128]{0:T(128)S(1)} %get-tuple-element.290, f32[1024]{0:T(1024)S(1)} %get-tuple-element.291, f32[128]{0:T(128)S(1)} %get-tuple-element.288, f32[1024]{0:T(1024)S(1)} %get-tuple-element.289, f32[128]{0:T(128)S(1)} %get-tuple-element.286, ...), kind=kLoop, calls=%fused_computation.6.clone.1 | loop fusion | flops 1310720 | bytes 542212 | tf_op jit(solution)/shard_map/convert
  9.2 1.4 %fusion.190 = f32[2,2,32,2,128]{4,2,3,1,0:T(8,128)S(1)} fusion(bf16[2,128,1024,1,1]{2,1,0,4,3:T(8,128)(2,1)S(1)} %bitcast.78, s32[16,2,2,32,1024]{4,3,2,1,0:T(8,128)} %get-tuple-element.284, s32[]{:T(128)S(6)} %copy.19), kind=kOutput, calls=%fused_computation.10.clone.1 | convolution fusion | flops 67239936 | bytes 1179652 | tf_op jit(solution)/shard_map/while/body/eval_jaxpr/dot_general | solution.py:30
  11.4 2.2 %fusion.189 = (bf16[1024,128]{0,1:T(8,128)(2,1)S(1)}, bf16[1024,128]{0,1:T(8,128)(2,1)S(1)}) fusion(f32[128]{0:T(128)S(1)} %get-tuple-element.290, f32[1024]{0:T(1024)S(1)} %get-tuple-element.291, f32[128]{0:T(128)S(1)} %get-tuple-element.288, f32[1024]{0:T(1024)S(1)} %get-tuple-element.289, f32[128]{0:T(128)S(1)} %get-tuple-element.286, ...), kind=kLoop, calls=%fused_computation.6.clone.1 | loop fusion | flops 1310720 | bytes 542212 | tf_op jit(solution)/shard_map/convert
  13.6 1.4 %fusion.190 = f32[2,2,32,2,128]{4,2,3,1,0:T(8,128)S(1)} fusion(bf16[2,128,1024,1,1]{2,1,0,4,3:T(8,128)(2,1)S(1)} %bitcast.78, s32[16,2,2,32,1024]{4,3,2,1,0:T(8,128)} %get-tuple-element.284, s32[]{:T(128)S(6)} %copy.19), kind=kOutput, calls=%fused_computation.10.clone.1 | convolution fusion | flops 67239936 | bytes 1179652 | tf_op jit(solution)/shard_map/while/body/eval_jaxpr/dot_general | solution.py:30
  15.9 2.2 %fusion.189 = (bf16[1024,128]{0,1:T(8,128)(2,1)S(1)}, bf16[1024,128]{0,1:T(8,128)(2,1)S(1)}) fusion(f32[128]{0:T(128)S(1)} %get-tuple-element.290, f32[1024]{0:T(1024)S(1)} %get-tuple-element.291, f32[128]{0:T(128)S(1)} %get-tuple-element.288, f32[1024]{0:T(1024)S(1)} %get-tuple-element.289, f32[128]{0:T(128)S(1)} %get-tuple-element.286, ...), kind=kLoop, calls=%fused_computation.6.clone.1 | loop fusion | flops 1310720 | bytes 542212 | tf_op jit(solution)/shard_map/convert
  18.1 1.4 %fusion.190 = f32[2,2,32,2,128]{4,2,3,1,0:T(8,128)S(1)} fusion(bf16[2,128,1024,1,1]{2,1,0,4,3:T(8,128)(2,1)S(1)} %bitcast.78, s32[16,2,2,32,1024]{4,3,2,1,0:T(8,128)} %get-tuple-element.284, s32[]{:T(128)S(6)} %copy.19), kind=kOutput, calls=%fused_computation.10.clone.1 | convolution fusion | flops 67239936 | bytes 1179652 | tf_op jit(solution)/shard_map/while/body/eval_jaxpr/dot_general | solution.py:30
  20.3 2.2 %fusion.189 = (bf16[1024,128]{0,1:T(8,128)(2,1)S(1)}, bf16[1024,128]{0,1:T(8,128)(2,1)S(1)}) fusion(f32[128]{0:T(128)S(1)} %get-tuple-element.290, f32[1024]{0:T(1024)S(1)} %get-tuple-element.291, f32[128]{0:T(128)S(1)} %get-tuple-element.288, f32[1024]{0:T(1024)S(1)} %get-tuple-element.289, f32[128]{0:T(128)S(1)} %get-tuple-element.286, ...), kind=kLoop, calls=%fused_computation.6.clone.1 | loop fusion | flops 1310720 | bytes 542212 | tf_op jit(solution)/shard_map/convert
  22.6 1.4 %fusion.190 = f32[2,2,32,2,128]{4,2,3,1,0:T(8,128)S(1)} fusion(bf16[2,128,1024,1,1]{2,1,0,4,3:T(8,128)(2,1)S(1)} %bitcast.78, s32[16,2,2,32,1024]{4,3,2,1,0:T(8,128)} %get-tuple-element.284, s32[]{:T(128)S(6)} %copy.19), kind=kOutput, calls=%fused_computation.10.clone.1 | convolution fusion | flops 67239936 | bytes 1179652 | tf_op jit(solution)/shard_map/while/body/eval_jaxpr/dot_general | solution.py:30
  24.8 2.2 %fusion.189 = (bf16[1024,128]{0,1:T(8,128)(2,1)S(1)}, bf16[1024,128]{0,1:T(8,128)(2,1)S(1)}) fusion(f32[128]{0:T(128)S(1)} %get-tuple-element.290, f32[1024]{0:T(1024)S(1)} %get-tuple-element.291, f32[128]{0:T(128)S(1)} %get-tuple-element.288, f32[1024]{0:T(1024)S(1)} %get-tuple-element.289, f32[128]{0:T(128)S(1)} %get-tuple-element.286, ...), kind=kLoop, calls=%fused_computation.6.clone.1 | loop fusion | flops 1310720 | bytes 542212 | tf_op jit(solution)/shard_map/convert
  29.3 2.2 %fusion.189 = (bf16[1024,128]{0,1:T(8,128)(2,1)S(1)}, bf16[1024,128]{0,1:T(8,128)(2,1)S(1)}) fusion(f32[128]{0:T(128)S(1)} %get-tuple-element.290, f32[1024]{0:T(1024)S(1)} %get-tuple-element.291, f32[128]{0:T(128)S(1)} %get-tuple-element.288, f32[1024]{0:T(1024)S(1)} %get-tuple-element.289, f32[128]{0:T(128)S(1)} %get-tuple-element.286, ...), kind=kLoop, calls=%fused_computation.6.clone.1 | loop fusion | flops 1310720 | bytes 542212 | tf_op jit(solution)/shard_map/convert
  31.5 1.4 %fusion.190 = f32[2,2,32,2,128]{4,2,3,1,0:T(8,128)S(1)} fusion(bf16[2,128,1024,1,1]{2,1,0,4,3:T(8,128)(2,1)S(1)} %bitcast.78, s32[16,2,2,32,1024]{4,3,2,1,0:T(8,128)} %get-tuple-element.284, s32[]{:T(128)S(6)} %copy.19), kind=kOutput, calls=%fused_computation.10.clone.1 | convolution fusion | flops 67239936 | bytes 1179652 | tf_op jit(solution)/shard_map/while/body/eval_jaxpr/dot_general | solution.py:30
  33.7 2.2 %fusion.189 = (bf16[1024,128]{0,1:T(8,128)(2,1)S(1)}, bf16[1024,128]{0,1:T(8,128)(2,1)S(1)}) fusion(f32[128]{0:T(128)S(1)} %get-tuple-element.290, f32[1024]{0:T(1024)S(1)} %get-tuple-element.291, f32[128]{0:T(128)S(1)} %get-tuple-element.288, f32[1024]{0:T(1024)S(1)} %get-tuple-element.289, f32[128]{0:T(128)S(1)} %get-tuple-element.286, ...), kind=kLoop, calls=%fused_computation.6.clone.1 | loop fusion | flops 1310720 | bytes 542212 | tf_op jit(solution)/shard_map/convert
  36.0 1.4 %fusion.190 = f32[2,2,32,2,128]{4,2,3,1,0:T(8,128)S(1)} fusion(bf16[2,128,1024,1,1]{2,1,0,4,3:T(8,128)(2,1)S(1)} %bitcast.78, s32[16,2,2,32,1024]{4,3,2,1,0:T(8,128)} %get-tuple-element.284, s32[]{:T(128)S(6)} %copy.19), kind=kOutput, calls=%fused_computation.10.clone.1 | convolution fusion | flops 67239936 | bytes 1179652 | tf_op jit(solution)/shard_map/while/body/eval_jaxpr/dot_general | solution.py:30
  38.2 2.2 %fusion.189 = (bf16[1024,128]{0,1:T(8,128)(2,1)S(1)}, bf16[1024,128]{0,1:T(8,128)(2,1)S(1)}) fusion(f32[128]{0:T(128)S(1)} %get-tuple-element.290, f32[1024]{0:T(1024)S(1)} %get-tuple-element.291, f32[128]{0:T(128)S(1)} %get-tuple-element.288, f32[1024]{0:T(1024)S(1)} %get-tuple-element.289, f32[128]{0:T(128)S(1)} %get-tuple-element.286, ...), kind=kLoop, calls=%fused_computation.6.clone.1 | loop fusion | flops 1310720 | bytes 542212 | tf_op jit(solution)/shard_map/convert
  40.5 1.4 %fusion.190 = f32[2,2,32,2,128]{4,2,3,1,0:T(8,128)S(1)} fusion(bf16[2,128,1024,1,1]{2,1,0,4,3:T(8,128)(2,1)S(1)} %bitcast.78, s32[16,2,2,32,1024]{4,3,2,1,0:T(8,128)} %get-tuple-element.284, s32[]{:T(128)S(6)} %copy.19), kind=kOutput, calls=%fused_computation.10.clone.1 | convolution fusion | flops 67239936 | bytes 1179652 | tf_op jit(solution)/shard_map/while/body/eval_jaxpr/dot_general | solution.py:30
  42.7 2.2 %fusion.189 = (bf16[1024,128]{0,1:T(8,128)(2,1)S(1)}, bf16[1024,128]{0,1:T(8,128)(2,1)S(1)}) fusion(f32[128]{0:T(128)S(1)} %get-tuple-element.290, f32[1024]{0:T(1024)S(1)} %get-tuple-element.291, f32[128]{0:T(128)S(1)} %get-tuple-element.288, f32[1024]{0:T(1024)S(1)} %get-tuple-element.289, f32[128]{0:T(128)S(1)} %get-tuple-element.286, ...), kind=kLoop, calls=%fused_computation.6.clone.1 | loop fusion | flops 1310720 | bytes 542212 | tf_op jit(solution)/shard_map/convert
  47.2 2.2 %fusion.189 = (bf16[1024,128]{0,1:T(8,128)(2,1)S(1)}, bf16[1024,128]{0,1:T(8,128)(2,1)S(1)}) fusion(f32[128]{0:T(128)S(1)} %get-tuple-element.290, f32[1024]{0:T(1024)S(1)} %get-tuple-element.291, f32[128]{0:T(128)S(1)} %get-tuple-element.288, f32[1024]{0:T(1024)S(1)} %get-tuple-element.289, f32[128]{0:T(128)S(1)} %get-tuple-element.286, ...), kind=kLoop, calls=%fused_computation.6.clone.1 | loop fusion | flops 1310720 | bytes 542212 | tf_op jit(solution)/shard_map/convert
  49.4 1.4 %fusion.190 = f32[2,2,32,2,128]{4,2,3,1,0:T(8,128)S(1)} fusion(bf16[2,128,1024,1,1]{2,1,0,4,3:T(8,128)(2,1)S(1)} %bitcast.78, s32[16,2,2,32,1024]{4,3,2,1,0:T(8,128)} %get-tuple-element.284, s32[]{:T(128)S(6)} %copy.19), kind=kOutput, calls=%fused_computation.10.clone.1 | convolution fusion | flops 67239936 | bytes 1179652 | tf_op jit(solution)/shard_map/while/body/eval_jaxpr/dot_general | solution.py:30
  51.6 2.2 %fusion.189 = (bf16[1024,128]{0,1:T(8,128)(2,1)S(1)}, bf16[1024,128]{0,1:T(8,128)(2,1)S(1)}) fusion(f32[128]{0:T(128)S(1)} %get-tuple-element.290, f32[1024]{0:T(1024)S(1)} %get-tuple-element.291, f32[128]{0:T(128)S(1)} %get-tuple-element.288, f32[1024]{0:T(1024)S(1)} %get-tuple-element.289, f32[128]{0:T(128)S(1)} %get-tuple-element.286, ...), kind=kLoop, calls=%fused_computation.6.clone.1 | loop fusion | flops 1310720 | bytes 542212 | tf_op jit(solution)/shard_map/convert
  56.1 2.2 %fusion.189 = (bf16[1024,128]{0,1:T(8,128)(2,1)S(1)}, bf16[1024,128]{0,1:T(8,128)(2,1)S(1)}) fusion(f32[128]{0:T(128)S(1)} %get-tuple-element.290, f32[1024]{0:T(1024)S(1)} %get-tuple-element.291, f32[128]{0:T(128)S(1)} %get-tuple-element.288, f32[1024]{0:T(1024)S(1)} %get-tuple-element.289, f32[128]{0:T(128)S(1)} %get-tuple-element.286, ...), kind=kLoop, calls=%fused_computation.6.clone.1 | loop fusion | flops 1310720 | bytes 542212 | tf_op jit(solution)/shard_map/convert
  60.6 2.2 %fusion.189 = (bf16[1024,128]{0,1:T(8,128)(2,1)S(1)}, bf16[1024,128]{0,1:T(8,128)(2,1)S(1)}) fusion(f32[128]{0:T(128)S(1)} %get-tuple-element.290, f32[1024]{0:T(1024)S(1)} %get-tuple-element.291, f32[128]{0:T(128)S(1)} %get-tuple-element.288, f32[1024]{0:T(1024)S(1)} %get-tuple-element.289, f32[128]{0:T(128)S(1)} %get-tuple-element.286, ...), kind=kLoop, calls=%fused_computation.6.clone.1 | loop fusion | flops 1310720 | bytes 542212 | tf_op jit(solution)/shard_map/convert
  65.0 2.2 %fusion.189 = (bf16[1024,128]{0,1:T(8,128)(2,1)S(1)}, bf16[1024,128]{0,1:T(8,128)(2,1)S(1)}) fusion(f32[128]{0:T(128)S(1)} %get-tuple-element.290, f32[1024]{0:T(1024)S(1)} %get-tuple-element.291, f32[128]{0:T(128)S(1)} %get-tuple-element.288, f32[1024]{0:T(1024)S(1)} %get-tuple-element.289, f32[128]{0:T(128)S(1)} %get-tuple-element.286, ...), kind=kLoop, calls=%fused_computation.6.clone.1 | loop fusion | flops 1310720 | bytes 542212 | tf_op jit(solution)/shard_map/convert
  67.3 1.4 %fusion.190 = f32[2,2,32,2,128]{4,2,3,1,0:T(8,128)S(1)} fusion(bf16[2,128,1024,1,1]{2,1,0,4,3:T(8,128)(2,1)S(1)} %bitcast.78, s32[16,2,2,32,1024]{4,3,2,1,0:T(8,128)} %get-tuple-element.284, s32[]{:T(128)S(6)} %copy.19), kind=kOutput, calls=%fused_computation.10.clone.1 | convolution fusion | flops 67239936 | bytes 1179652 | tf_op jit(solution)/shard_map/while/body/eval_jaxpr/dot_general | solution.py:30
  69.5 2.2 %fusion.189 = (bf16[1024,128]{0,1:T(8,128)(2,1)S(1)}, bf16[1024,128]{0,1:T(8,128)(2,1)S(1)}) fusion(f32[128]{0:T(128)S(1)} %get-tuple-element.290, f32[1024]{0:T(1024)S(1)} %get-tuple-element.291, f32[128]{0:T(128)S(1)} %get-tuple-element.288, f32[1024]{0:T(1024)S(1)} %get-tuple-element.289, f32[128]{0:T(128)S(1)} %get-tuple-element.286, ...), kind=kLoop, calls=%fused_computation.6.clone.1 | loop fusion | flops 1310720 | bytes 542212 | tf_op jit(solution)/shard_map/convert
  71.8 1.4 %fusion.190 = f32[2,2,32,2,128]{4,2,3,1,0:T(8,128)S(1)} fusion(bf16[2,128,1024,1,1]{2,1,0,4,3:T(8,128)(2,1)S(1)} %bitcast.78, s32[16,2,2,32,1024]{4,3,2,1,0:T(8,128)} %get-tuple-element.284, s32[]{:T(128)S(6)} %copy.19), kind=kOutput, calls=%fused_computation.10.clone.1 | convolution fusion | flops 67239936 | bytes 1179652 | tf_op jit(solution)/shard_map/while/body/eval_jaxpr/dot_general | solution.py:30
  74.1 1.8 %reshape.148 = bf16[16,2,2048]{2,1,0:T(2,128)(2,1)} reshape(bf16[16,16,16,16]{3,2,1,0:T(8,128)(2,1)S(1)} %bitcast.81) | data formatting | bytes 262144
  75.8 7.4 %all-to-all-start = ((bf16[16,2,2048]{2,1,0:T(2,128)(2,1)}), bf16[16,2,2048]{2,1,0:T(2,128)(2,1)S(1)}, u32[]{:S(2)}, u32[]{:S(2)}) async-start(bf16[16,2,2048]{2,1,0:T(2,128)(2,1)} %reshape.148), calls=%async_computation | async-start | bytes 262144 | tf_op jit(solution)/shard_map/all_to_all | solution.py:91
  83.3 7.8 %all-to-all-done = bf16[16,2,2048]{2,1,0:T(2,128)(2,1)S(1)} async-done(((bf16[16,2,2048]{2,1,0:T(2,128)(2,1)}), bf16[16,2,2048]{2,1,0:T(2,128)(2,1)S(1)}, u32[]{:S(2)}, u32[]{:S(2)}) %all-to-all-start) | async-done | bytes 131104 | tf_op jit(solution)/shard_map/all_to_all | solution.py:91
  95.4 8.3 %collective-permute-done = bf16[256,15,16]{0,2,1:T(8,128)(2,1)S(1)} collective-permute-done((bf16[256,15,16]{0,2,1:T(8,128)(2,1)S(1)}, bf16[256,15,16]{0,2,1:T(8,128)(2,1)S(1)}, u32[]{:S(2)}, u32[]{:S(2)}) %collective-permute-start) | collective-permute-done | bytes 122912 | tf_op jit(solution)/shard_map/ppermute | solution.py:15
  (133 shorter events, 35.1 us)
Async XLA Ops:
  1.6 93.3 %copy-start = (s32[256]{0:T(256)S(1)}, s32[256]{0:T(256)}, u32[]{:S(2)}) copy-start(s32[256]{0:T(256)} %param.11) | copy-start | bytes 3076
  75.8 15.3 %all-to-all-start = ((bf16[16,2,2048]{2,1,0:T(2,128)(2,1)}), bf16[16,2,2048]{2,1,0:T(2,128)(2,1)S(1)}, u32[]{:S(2)}, u32[]{:S(2)}) async-start(bf16[16,2,2048]{2,1,0:T(2,128)(2,1)} %reshape.148), calls=%async_computation | async-start | bytes 262144 | tf_op jit(solution)/shard_map/all_to_all | solution.py:91
  93.7 10.0 %collective-permute-start = (bf16[256,15,16]{0,2,1:T(8,128)(2,1)S(1)}, bf16[256,15,16]{0,2,1:T(8,128)(2,1)S(1)}, u32[]{:S(2)}, u32[]{:S(2)}) collective-permute-start(bf16[256,15,16]{0,2,1:T(8,128)(2,1)S(1)} %slice.144), channel_id=1, source_target_pairs={{8,0},{9,1},{10,2},{11,3},{12,4},{13,5},{14,6},{15,7},{24,16},{25,... | collective-permute-start | bytes 368648 | tf_op jit(solution)/shard_map/ppermute | solution.py:15
where the time goes:
time: 113 us; the launch traced here: 111 us
  other arithmetic  49.3 us (44%)
  matrix products  28.6 us (25%)
  waiting for transfers between devices  16.1 us (14%)
  starting transfers between devices  8.67 us (8%)
  local copies, waits for them, and re-layouts  7.75 us (7%)
    another operation x16, other arithmetic  35.1 us
    dot_general x16, matrix products, channel_flat(): jnp.dot(row_block, weight_pair, preferred_element_type=jnp.float32)  21.7 us
    convert_element_type x16, other arithmetic, channel_flat(): scale_col = scale_chan.astype(jnp.float32)[:, None]  12.3 us
    ppermute x1, waiting for transfers between devices, passed_along(): lax.ppermute(value, axis, [(source, source + steps) for source in range(l...  8.26 us
    all_to_all x1, waiting for transfers between devices, local(): lax.all_to_all(outgoing, 'chan', split_axis=0, concat_axis=0, tiled=True)  7.81 us
    all_to_all x1, starting transfers between devices, local(): lax.all_to_all(outgoing, 'chan', split_axis=0, concat_axis=0, tiled=True)  7.38 us
    dot_general x16, matrix products, dedisperse(): jnp.dot(onehots[shift_step], segment, preferred_element_type=jnp.float32)  6.9 us
    unnamed x4, local copies, waits for them, and re-layouts  2.46 us
  transfers between devices with their start and end apart: 2, of which 2 were waited for; matrix products, arithmetic and copies ran while one was open for 0% of the time, Pallas kernels for 0%

commit v1 on v0

--- a/solution.py
+++ b/solution.py
@@ -7,6 +7,28 @@
 MAXD = 15
 TWO_PI = 6.283185307179586
 POWER_SCALE = 1.0 / 67108864.0
+
+
+def cut_along(x, dim, peers):
+    before, after = (x.shape[:dim], x.shape[dim + 1 :])
+    return jnp.moveaxis(x.reshape(*before, peers, -1, *after), dim, 0)
+
+
+def in_order(pieces, dim):
+    shape = list(pieces.shape[1:])
+    shape[dim] *= pieces.shape[0]
+    return jnp.moveaxis(pieces, 0, dim).reshape(shape)
+
+
+def pairwise_exchange(x, axis, split_dim, concat_dim):
+    devices, index = (lax.axis_size(axis), lax.axis_index(axis))
+    parts = cut_along(x, split_dim, devices)
+    gathered = [parts[index]]
+    for step in range(1, devices):
+        sent = parts[index ^ step]
+        gathered.append(lax.ppermute(sent, axis, [(i, i ^ step) for i in range(devices)]))
+    parts = jnp.stack(gathered)[index ^ jnp.arange(devices)]
+    return in_order(parts, concat_dim)
 
 
 def passed_along(value, axis, steps):
@@ -88,7 +110,7 @@
     outgoing = outgoing.transpose(1, 3, 0, 2, 4).reshape(
         groups, chan_local, time_steps, block_beams
     )
-    arrived = lax.all_to_all(outgoing, "chan", split_axis=0, concat_axis=0, tiled=True)
+    arrived = pairwise_exchange(outgoing, "chan", 0, 0)
     arrived_block = arrived.reshape(chan_total, time_steps, arrived.shape[3])
     tail_rows = passed_along(arrived_block[:, :MAXD, :], "chan", -half_groups)
     extended = jnp.concatenate([arrived_block, tail_rows], axis=1)

time: 113 us -> 132 us (1.17)
  starting transfers between devices: 8.67 us -> 26.9 us
  waiting for transfers between devices: 16.1 us -> 17.7 us
    ppermute x0 -> x15, starting transfers between devices: none -> 25.4 us  [pairwise_exchange(): lax.ppermute(sent, axis, [(i, i ^ step) for i in range(devices)])]
    all_to_all x1 -> x0, waiting for transfers between devices: 7.81 us -> none  [local(): lax.all_to_all(outgoing, 'chan', split_axis=0, concat_axis=0, tiled=True)]
    ppermute x0 -> x15, waiting for transfers between devices: none -> 7.55 us  [pairwise_exchange(): lax.ppermute(sent, axis, [(i, i ^ step) for i in range(devices)])]
    all_to_all x1 -> x0, starting transfers between devices: 7.38 us -> none  [local(): lax.all_to_all(outgoing, 'chan', split_axis=0, concat_axis=0, tiled=True)]
    unnamed x4 -> x16, local copies, waits for them, and re-layouts: 2.46 us -> 0.19 us
    ppermute x1, waiting for transfers between devices: 8.26 us -> 10.1 us  [passed_along(): lax.ppermute(value, axis, [(source, source + steps) for source in range(l...]
  transfers between devices with their start and end apart: 2 -> 16, of which waited for: 2 -> 4; matrix products, arithmetic and copies ran while one was open for 0% -> 1% of each run, Pallas kernels for 0% -> 0%
where the time goes in v1:
time: 132 us; the launch traced here: 130 us
  other arithmetic  49.3 us (37%)
  matrix products  28.6 us (22%)
  starting transfers between devices  26.9 us (20%)
  waiting for transfers between devices  17.7 us (13%)
  local copies, waits for them, and re-layouts  6.53 us (5%)
    another operation x16, other arithmetic  35.1 us
    ppermute x15, starting transfers between devices, pairwise_exchange(): lax.ppermute(sent, axis, [(i, i ^ step) for i in range(devices)])  25.4 us
    dot_general x16, matrix products, channel_flat(): jnp.dot(row_block, weight_pair, preferred_element_type=jnp.float32)  21.7 us
    convert_element_type x16, other arithmetic, channel_flat(): scale_col = scale_chan.astype(jnp.float32)[:, None]  12.3 us
    ppermute x1, waiting for transfers between devices, passed_along(): lax.ppermute(value, axis, [(source, source + steps) for source in range(l...  10.1 us
    ppermute x15, waiting for transfers between devices, pairwise_exchange(): lax.ppermute(sent, axis, [(i, i ^ step) for i in range(devices)])  7.55 us
    dot_general x16, matrix products, dedisperse(): jnp.dot(onehots[shift_step], segment, preferred_element_type=jnp.float32)  6.9 us
  transfers between devices with their start and end apart: 16, of which 4 were waited for; matrix products, arithmetic and copies ran while one was open for 1% of the time, Pallas kernels for 0%

profile of v1, /device:TPU:0, one launch (start us, length us, event | category | flops | bytes accessed | tf_op | source)
XLA Modules:
  0.0 130.1 jit_solution(9538436267019791826)
XLA Ops:
  1.6 71.5 %while.12 = (s32[]{:T(128)}, bf16[16,32,128]{2,1,0:T(8,128)(2,1)S(1)}, s32[16,2,2,32,1024]{4,3,2,1,0:T(8,128)}, s32[16,1024]{1,0:T(8,128)}, f32[128]{0:T(128)S(1...) while((s32[]{:T(128)}, ...), condition=%wide.region_2.3_spmd.clone.clone, body=%wide.region_0.2_spmd.clone.clone.sunk | while | flops 69661696 | bytes 3083917 | solution.py:106
  2.4 2.2 %fusion.190 = (bf16[1024,128]{0,1:T(8,128)(2,1)S(1)}, bf16[1024,128]{0,1:T(8,128)(2,1)S(1)}) fusion(f32[128]{0:T(128)S(1)} %get-tuple-element.306, f32[1024]{0:T(1024)S(1)} %get-tuple-element.307, f32[128]{0:T(128)S(1)} %get-tuple-element.304, f32[1024]{0:T(1024)S(1)} %get-tuple-element.305, f32[128]{0:T(128)S(1)} %get-tuple-element.302, ...), kind=kLoop, calls=%fused_computation.7.clone.1 | loop fusion | flops 1310720 | bytes 542212 | tf_op jit(solution)/shard_map/convert
  6.9 2.2 %fusion.190 = (bf16[1024,128]{0,1:T(8,128)(2,1)S(1)}, bf16[1024,128]{0,1:T(8,128)(2,1)S(1)}) fusion(f32[128]{0:T(128)S(1)} %get-tuple-element.306, f32[1024]{0:T(1024)S(1)} %get-tuple-element.307, f32[128]{0:T(128)S(1)} %get-tuple-element.304, f32[1024]{0:T(1024)S(1)} %get-tuple-element.305, f32[128]{0:T(128)S(1)} %get-tuple-element.302, ...), kind=kLoop, calls=%fused_computation.7.clone.1 | loop fusion | flops 1310720 | bytes 542212 | tf_op jit(solution)/shard_map/convert
  11.4 2.2 %fusion.190 = (bf16[1024,128]{0,1:T(8,128)(2,1)S(1)}, bf16[1024,128]{0,1:T(8,128)(2,1)S(1)}) fusion(f32[128]{0:T(128)S(1)} %get-tuple-element.306, f32[1024]{0:T(1024)S(1)} %get-tuple-element.307, f32[128]{0:T(128)S(1)} %get-tuple-element.304, f32[1024]{0:T(1024)S(1)} %get-tuple-element.305, f32[128]{0:T(128)S(1)} %get-tuple-element.302, ...), kind=kLoop, calls=%fused_computation.7.clone.1 | loop fusion | flops 1310720 | bytes 542212 | tf_op jit(solution)/shard_map/convert
  15.8 2.2 %fusion.190 = (bf16[1024,128]{0,1:T(8,128)(2,1)S(1)}, bf16[1024,128]{0,1:T(8,128)(2,1)S(1)}) fusion(f32[128]{0:T(128)S(1)} %get-tuple-element.306, f32[1024]{0:T(1024)S(1)} %get-tuple-element.307, f32[128]{0:T(128)S(1)} %get-tuple-element.304, f32[1024]{0:T(1024)S(1)} %get-tuple-element.305, f32[128]{0:T(128)S(1)} %get-tuple-element.302, ...), kind=kLoop, calls=%fused_computation.7.clone.1 | loop fusion | flops 1310720 | bytes 542212 | tf_op jit(solution)/shard_map/convert
  18.1 1.4 %fusion.191 = f32[2,2,32,2,128]{4,2,3,1,0:T(8,128)S(1)} fusion(bf16[2,128,1024,1,1]{2,1,0,4,3:T(8,128)(2,1)S(1)} %bitcast.141, s32[16,2,2,32,1024]{4,3,2,1,0:T(8,128)} %get-tuple-element.300, s32[]{:T(128)S(6)} %copy.19), kind=kOutput, calls=%fused_computation.11.clone.1 | convolution fusion | flops 67239936 | bytes 1179652 | tf_op jit(solution)/shard_map/while/body/eval_jaxpr/dot_general | solution.py:52
  20.3 2.2 %fusion.190 = (bf16[1024,128]{0,1:T(8,128)(2,1)S(1)}, bf16[1024,128]{0,1:T(8,128)(2,1)S(1)}) fusion(f32[128]{0:T(128)S(1)} %get-tuple-element.306, f32[1024]{0:T(1024)S(1)} %get-tuple-element.307, f32[128]{0:T(128)S(1)} %get-tuple-element.304, f32[1024]{0:T(1024)S(1)} %get-tuple-element.305, f32[128]{0:T(128)S(1)} %get-tuple-element.302, ...), kind=kLoop, calls=%fused_computation.7.clone.1 | loop fusion | flops 1310720 | bytes 542212 | tf_op jit(solution)/shard_map/convert
  22.6 1.4 %fusion.191 = f32[2,2,32,2,128]{4,2,3,1,0:T(8,128)S(1)} fusion(bf16[2,128,1024,1,1]{2,1,0,4,3:T(8,128)(2,1)S(1)} %bitcast.141, s32[16,2,2,32,1024]{4,3,2,1,0:T(8,128)} %get-tuple-element.300, s32[]{:T(128)S(6)} %copy.19), kind=kOutput, calls=%fused_computation.11.clone.1 | convolution fusion | flops 67239936 | bytes 1179652 | tf_op jit(solution)/shard_map/while/body/eval_jaxpr/dot_general | solution.py:52
  24.8 2.2 %fusion.190 = (bf16[1024,128]{0,1:T(8,128)(2,1)S(1)}, bf16[1024,128]{0,1:T(8,128)(2,1)S(1)}) fusion(f32[128]{0:T(128)S(1)} %get-tuple-element.306, f32[1024]{0:T(1024)S(1)} %get-tuple-element.307, f32[128]{0:T(128)S(1)} %get-tuple-element.304, f32[1024]{0:T(1024)S(1)} %get-tuple-element.305, f32[128]{0:T(128)S(1)} %get-tuple-element.302, ...), kind=kLoop, calls=%fused_computation.7.clone.1 | loop fusion | flops 1310720 | bytes 542212 | tf_op jit(solution)/shard_map/convert
  27.0 1.4 %fusion.191 = f32[2,2,32,2,128]{4,2,3,1,0:T(8,128)S(1)} fusion(bf16[2,128,1024,1,1]{2,1,0,4,3:T(8,128)(2,1)S(1)} %bitcast.141, s32[16,2,2,32,1024]{4,3,2,1,0:T(8,128)} %get-tuple-element.300, s32[]{:T(128)S(6)} %copy.19), kind=kOutput, calls=%fused_computation.11.clone.1 | convolution fusion | flops 67239936 | bytes 1179652 | tf_op jit(solution)/shard_map/while/body/eval_jaxpr/dot_general | solution.py:52
  29.3 2.2 %fusion.190 = (bf16[1024,128]{0,1:T(8,128)(2,1)S(1)}, bf16[1024,128]{0,1:T(8,128)(2,1)S(1)}) fusion(f32[128]{0:T(128)S(1)} %get-tuple-element.306, f32[1024]{0:T(1024)S(1)} %get-tuple-element.307, f32[128]{0:T(128)S(1)} %get-tuple-element.304, f32[1024]{0:T(1024)S(1)} %get-tuple-element.305, f32[128]{0:T(128)S(1)} %get-tuple-element.302, ...), kind=kLoop, calls=%fused_computation.7.clone.1 | loop fusion | flops 1310720 | bytes 542212 | tf_op jit(solution)/shard_map/convert
  33.7 2.2 %fusion.190 = (bf16[1024,128]{0,1:T(8,128)(2,1)S(1)}, bf16[1024,128]{0,1:T(8,128)(2,1)S(1)}) fusion(f32[128]{0:T(128)S(1)} %get-tuple-element.306, f32[1024]{0:T(1024)S(1)} %get-tuple-element.307, f32[128]{0:T(128)S(1)} %get-tuple-element.304, f32[1024]{0:T(1024)S(1)} %get-tuple-element.305, f32[128]{0:T(128)S(1)} %get-tuple-element.302, ...), kind=kLoop, calls=%fused_computation.7.clone.1 | loop fusion | flops 1310720 | bytes 542212 | tf_op jit(solution)/shard_map/convert
  38.2 2.2 %fusion.190 = (bf16[1024,128]{0,1:T(8,128)(2,1)S(1)}, bf16[1024,128]{0,1:T(8,128)(2,1)S(1)}) fusion(f32[128]{0:T(128)S(1)} %get-tuple-element.306, f32[1024]{0:T(1024)S(1)} %get-tuple-element.307, f32[128]{0:T(128)S(1)} %get-tuple-element.304, f32[1024]{0:T(1024)S(1)} %get-tuple-element.305, f32[128]{0:T(128)S(1)} %get-tuple-element.302, ...), kind=kLoop, calls=%fused_computation.7.clone.1 | loop fusion | flops 1310720 | bytes 542212 | tf_op jit(solution)/shard_map/convert
  42.7 2.2 %fusion.190 = (bf16[1024,128]{0,1:T(8,128)(2,1)S(1)}, bf16[1024,128]{0,1:T(8,128)(2,1)S(1)}) fusion(f32[128]{0:T(128)S(1)} %get-tuple-element.306, f32[1024]{0:T(1024)S(1)} %get-tuple-element.307, f32[128]{0:T(128)S(1)} %get-tuple-element.304, f32[1024]{0:T(1024)S(1)} %get-tuple-element.305, f32[128]{0:T(128)S(1)} %get-tuple-element.302, ...), kind=kLoop, calls=%fused_computation.7.clone.1 | loop fusion | flops 1310720 | bytes 542212 | tf_op jit(solution)/shard_map/convert
  47.1 2.2 %fusion.190 = (bf16[1024,128]{0,1:T(8,128)(2,1)S(1)}, bf16[1024,128]{0,1:T(8,128)(2,1)S(1)}) fusion(f32[128]{0:T(128)S(1)} %get-tuple-element.306, f32[1024]{0:T(1024)S(1)} %get-tuple-element.307, f32[128]{0:T(128)S(1)} %get-tuple-element.304, f32[1024]{0:T(1024)S(1)} %get-tuple-element.305, f32[128]{0:T(128)S(1)} %get-tuple-element.302, ...), kind=kLoop, calls=%fused_computation.7.clone.1 | loop fusion | flops 1310720 | bytes 542212 | tf_op jit(solution)/shard_map/convert
  51.6 2.2 %fusion.190 = (bf16[1024,128]{0,1:T(8,128)(2,1)S(1)}, bf16[1024,128]{0,1:T(8,128)(2,1)S(1)}) fusion(f32[128]{0:T(128)S(1)} %get-tuple-element.306, f32[1024]{0:T(1024)S(1)} %get-tuple-element.307, f32[128]{0:T(128)S(1)} %get-tuple-element.304, f32[1024]{0:T(1024)S(1)} %get-tuple-element.305, f32[128]{0:T(128)S(1)} %get-tuple-element.302, ...), kind=kLoop, calls=%fused_computation.7.clone.1 | loop fusion | flops 1310720 | bytes 542212 | tf_op jit(solution)/shard_map/convert
  56.1 2.2 %fusion.190 = (bf16[1024,128]{0,1:T(8,128)(2,1)S(1)}, bf16[1024,128]{0,1:T(8,128)(2,1)S(1)}) fusion(f32[128]{0:T(128)S(1)} %get-tuple-element.306, f32[1024]{0:T(1024)S(1)} %get-tuple-element.307, f32[128]{0:T(128)S(1)} %get-tuple-element.304, f32[1024]{0:T(1024)S(1)} %get-tuple-element.305, f32[128]{0:T(128)S(1)} %get-tuple-element.302, ...), kind=kLoop, calls=%fused_computation.7.clone.1 | loop fusion | flops 1310720 | bytes 542212 | tf_op jit(solution)/shard_map/convert
  60.5 2.2 %fusion.190 = (bf16[1024,128]{0,1:T(8,128)(2,1)S(1)}, bf16[1024,128]{0,1:T(8,128)(2,1)S(1)}) fusion(f32[128]{0:T(128)S(1)} %get-tuple-element.306, f32[1024]{0:T(1024)S(1)} %get-tuple-element.307, f32[128]{0:T(128)S(1)} %get-tuple-element.304, f32[1024]{0:T(1024)S(1)} %get-tuple-element.305, f32[128]{0:T(128)S(1)} %get-tuple-element.302, ...), kind=kLoop, calls=%fused_computation.7.clone.1 | loop fusion | flops 1310720 | bytes 542212 | tf_op jit(solution)/shard_map/convert
  65.0 2.2 %fusion.190 = (bf16[1024,128]{0,1:T(8,128)(2,1)S(1)}, bf16[1024,128]{0,1:T(8,128)(2,1)S(1)}) fusion(f32[128]{0:T(128)S(1)} %get-tuple-element.306, f32[1024]{0:T(1024)S(1)} %get-tuple-element.307, f32[128]{0:T(128)S(1)} %get-tuple-element.304, f32[1024]{0:T(1024)S(1)} %get-tuple-element.305, f32[128]{0:T(128)S(1)} %get-tuple-element.302, ...), kind=kLoop, calls=%fused_computation.7.clone.1 | loop fusion | flops 1310720 | bytes 542212 | tf_op jit(solution)/shard_map/convert
  69.5 2.2 %fusion.190 = (bf16[1024,128]{0,1:T(8,128)(2,1)S(1)}, bf16[1024,128]{0,1:T(8,128)(2,1)S(1)}) fusion(f32[128]{0:T(128)S(1)} %get-tuple-element.306, f32[1024]{0:T(1024)S(1)} %get-tuple-element.307, f32[128]{0:T(128)S(1)} %get-tuple-element.304, f32[1024]{0:T(1024)S(1)} %get-tuple-element.305, f32[128]{0:T(128)S(1)} %get-tuple-element.302, ...), kind=kLoop, calls=%fused_computation.7.clone.1 | loop fusion | flops 1310720 | bytes 542212 | tf_op jit(solution)/shard_map/convert
  74.9 2.6 %collective-permute-start.1 = (bf16[1,16,16,16]{3,2,1,0:T(8,128)(2,1)S(1)}, bf16[1,16,16,16]{3,2,1,0:T(8,128)(2,1)S(1)}, u32[]{:S(2)}, u32[]{:S(2)}) collective-permute-start(bf16[1,16,16,16]{3,2,1,0:T(8,128)(2,1)S(1)} %get-tuple-element.171), channel_id=1, source_target_pairs={{0,2},{1,3},{2,0},{3,1},{4,6},{5,7},{6,4},{7,5},{8,10},{9,11},{10,... | collective-permute-start | bytes 24584 | tf_op jit(solution)/shard_map/ppermute | solution.py:29
  77.6 1.8 %collective-permute-start.3 = (bf16[1,16,16,16]{3,2,1,0:T(8,128)(2,1)S(1)}, bf16[1,16,16,16]{3,2,1,0:T(8,128)(2,1)S(1)}, u32[]{:S(2)}, u32[]{:S(2)}) collective-permute-start(bf16[1,16,16,16]{3,2,1,0:T(8,128)(2,1)S(1)} %get-tuple-element.169), channel_id=1, source_target_pairs={{0,4},{1,5},{2,6},{3,7},{4,0},{5,1},{6,2},{7,3},{8,12},{9,13},{10,... | collective-permute-start | bytes 24584 | tf_op jit(solution)/shard_map/ppermute | solution.py:29
  79.6 2.7 %collective-permute-start.5 = (bf16[1,16,16,16]{3,2,1,0:T(8,128)(2,1)S(1)}, bf16[1,16,16,16]{3,2,1,0:T(8,128)(2,1)S(1)}, u32[]{:S(2)}, u32[]{:S(2)}) collective-permute-start(bf16[1,16,16,16]{3,2,1,0:T(8,128)(2,1)S(1)} %get-tuple-element.167), channel_id=1, source_target_pairs={{0,6},{1,7},{2,4},{3,5},{4,2},{5,3},{6,0},{7,1},{8,14},{9,15},{10,... | collective-permute-start | bytes 24584 | tf_op jit(solution)/shard_map/ppermute | solution.py:29
  82.4 2.7 %collective-permute-start.7 = (bf16[1,16,16,16]{3,2,1,0:T(8,128)(2,1)S(1)}, bf16[1,16,16,16]{3,2,1,0:T(8,128)(2,1)S(1)}, u32[]{:S(2)}, u32[]{:S(2)}) collective-permute-start(bf16[1,16,16,16]{3,2,1,0:T(8,128)(2,1)S(1)} %get-tuple-element.165), channel_id=1, source_target_pairs={{0,8},{1,9},{2,10},{3,11},{4,12},{5,13},{6,14},{7,15},{8,0},{9,1},... | collective-permute-start | bytes 24584 | tf_op jit(solution)/shard_map/ppermute | solution.py:29
  86.0 2.9 %collective-permute-start.9 = (bf16[1,16,16,16]{3,2,1,0:T(8,128)(2,1)S(1)}, bf16[1,16,16,16]{3,2,1,0:T(8,128)(2,1)S(1)}, u32[]{:S(2)}, u32[]{:S(2)}) collective-permute-start(bf16[1,16,16,16]{3,2,1,0:T(8,128)(2,1)S(1)} %get-tuple-element.163), channel_id=1, source_target_pairs={{0,10},{1,11},{2,8},{3,9},{4,14},{5,15},{6,12},{7,13},{8,2},{9,3},... | collective-permute-start | bytes 24584 | tf_op jit(solution)/shard_map/ppermute | solution.py:29
  89.4 3.3 %collective-permute-start.11 = (bf16[1,16,16,16]{3,2,1,0:T(8,128)(2,1)S(1)}, bf16[1,16,16,16]{3,2,1,0:T(8,128)(2,1)S(1)}, u32[]{:S(2)}, u32[]{:S(2)}) collective-permute-start(bf16[1,16,16,16]{3,2,1,0:T(8,128)(2,1)S(1)} %get-tuple-element.161), channel_id=1, source_target_pairs={{0,12},{1,13},{2,14},{3,15},{4,8},{5,9},{6,10},{7,11},{8,4},{9,5},... | collective-permute-start | bytes 24584 | tf_op jit(solution)/shard_map/ppermute | solution.py:29
  93.4 3.6 %collective-permute-done.8 = bf16[1,16,16,16]{3,2,1,0:T(8,128)(2,1)S(1)} collective-permute-done((bf16[1,16,16,16]{3,2,1,0:T(8,128)(2,1)S(1)}, bf16[1,16,16,16]{3,2,1,0:T(8,128)(2,1)S(1)}, u32[]{:S(2)}, u32[]{:S(2)}) %collective-permute-start.8) | collective-permute-done | bytes 8224 | tf_op jit(solution)/shard_map/ppermute | solution.py:29
  97.0 3.6 %collective-permute-start.13 = (bf16[1,16,16,16]{3,2,1,0:T(8,128)(2,1)S(1)}, bf16[1,16,16,16]{3,2,1,0:T(8,128)(2,1)S(1)}, u32[]{:S(2)}, u32[]{:S(2)}) collective-permute-start(bf16[1,16,16,16]{3,2,1,0:T(8,128)(2,1)S(1)} %get-tuple-element.159), channel_id=1, source_target_pairs={{0,14},{1,15},{2,12},{3,13},{4,10},{5,11},{6,8},{7,9},{8,6},{9,7},... | collective-permute-start | bytes 24584 | tf_op jit(solution)/shard_map/ppermute | solution.py:29
  100.9 3.1 %collective-permute-start.14 = (bf16[1,16,16,16]{3,2,1,0:T(8,128)(2,1)S(1)}, bf16[1,16,16,16]{3,2,1,0:T(8,128)(2,1)S(1)}, u32[]{:S(2)}, u32[]{:S(2)}) collective-permute-start(bf16[1,16,16,16]{3,2,1,0:T(8,128)(2,1)S(1)} %get-tuple-element.158), channel_id=1, source_target_pairs={{0,15},{1,14},{2,13},{3,12},{4,11},{5,10},{6,9},{7,8},{8,7},{9,6},... | collective-permute-start | bytes 24584 | tf_op jit(solution)/shard_map/ppermute | solution.py:29
  104.2 3.7 %collective-permute-done.14 = bf16[1,16,16,16]{3,2,1,0:T(8,128)(2,1)S(1)} collective-permute-done((bf16[1,16,16,16]{3,2,1,0:T(8,128)(2,1)S(1)}, bf16[1,16,16,16]{3,2,1,0:T(8,128)(2,1)S(1)}, u32[]{:S(2)}, u32[]{:S(2)}) %collective-permute-start.14) | collective-permute-done | bytes 8224 | tf_op jit(solution)/shard_map/ppermute | solution.py:29
  110.5 1.5 %collective-permute-start.15 = (bf16[256,15,16]{0,2,1:T(8,128)(2,1)S(1)}, bf16[256,15,16]{0,2,1:T(8,128)(2,1)S(1)}, u32[]{:S(2)}, u32[]{:S(2)}) collective-permute-start(bf16[256,15,16]{0,2,1:T(8,128)(2,1)S(1)} %slice.146), channel_id=1, source_target_pairs={{8,0},{9,1},{10,2},{11,3},{12,4},{13,5},{14,6},{15,7},{24,16},{25,... | collective-permute-start | bytes 368648 | tf_op jit(solution)/shard_map/ppermute | solution.py:37
  112.4 10.1 %collective-permute-done.15 = bf16[256,15,16]{0,2,1:T(8,128)(2,1)S(1)} collective-permute-done((bf16[256,15,16]{0,2,1:T(8,128)(2,1)S(1)}, bf16[256,15,16]{0,2,1:T(8,128)(2,1)S(1)}, u32[]{:S(2)}, u32[]{:S(2)}) %collective-permute-start.15) | collective-permute-done | bytes 122912 | tf_op jit(solution)/shard_map/ppermute | solution.py:37
  (178 shorter events, 48.1 us)
Async XLA Ops:
  73.2 38.8 %copy-start = (s32[256]{0:T(256)S(1)}, s32[256]{0:T(256)}, u32[]{:S(2)}) copy-start(s32[256]{0:T(256)} %param.11) | copy-start | bytes 3076
  74.4 5.1 %collective-permute-start = (bf16[1,16,16,16]{3,2,1,0:T(8,128)(2,1)S(1)}, bf16[1,16,16,16]{3,2,1,0:T(8,128)(2,1)S(1)}, u32[]{:S(2)}, u32[]{:S(2)}) collective-permute-start(bf16[1,16,16,16]{3,2,1,0:T(8,128)(2,1)S(1)} %get-tuple-element.172), channel_id=1, source_target_pairs={{0,1},{1,0},{2,3},{3,2},{4,5},{5,4},{6,7},{7,6},{8,9},{9,8},{10,11... | collective-permute-start | bytes 24584 | tf_op jit(solution)/shard_map/ppermute | solution.py:29
  74.9 7.3 %collective-permute-start.1 = (bf16[1,16,16,16]{3,2,1,0:T(8,128)(2,1)S(1)}, bf16[1,16,16,16]{3,2,1,0:T(8,128)(2,1)S(1)}, u32[]{:S(2)}, u32[]{:S(2)}) collective-permute-start(bf16[1,16,16,16]{3,2,1,0:T(8,128)(2,1)S(1)} %get-tuple-element.171), channel_id=1, source_target_pairs={{0,2},{1,3},{2,0},{3,1},{4,6},{5,7},{6,4},{7,5},{8,10},{9,11},{10,... | collective-permute-start | bytes 24584 | tf_op jit(solution)/shard_map/ppermute | solution.py:29
  77.5 4.9 %collective-permute-start.2 = (bf16[1,16,16,16]{3,2,1,0:T(8,128)(2,1)S(1)}, bf16[1,16,16,16]{3,2,1,0:T(8,128)(2,1)S(1)}, u32[]{:S(2)}, u32[]{:S(2)}) collective-permute-start(bf16[1,16,16,16]{3,2,1,0:T(8,128)(2,1)S(1)} %get-tuple-element.170), channel_id=1, source_target_pairs={{0,3},{1,2},{2,1},{3,0},{4,7},{5,6},{6,5},{7,4},{8,11},{9,10},{10,... | collective-permute-start | bytes 24584 | tf_op jit(solution)/shard_map/ppermute | solution.py:29
  77.6 7.6 %collective-permute-start.3 = (bf16[1,16,16,16]{3,2,1,0:T(8,128)(2,1)S(1)}, bf16[1,16,16,16]{3,2,1,0:T(8,128)(2,1)S(1)}, u32[]{:S(2)}, u32[]{:S(2)}) collective-permute-start(bf16[1,16,16,16]{3,2,1,0:T(8,128)(2,1)S(1)} %get-tuple-element.169), channel_id=1, source_target_pairs={{0,4},{1,5},{2,6},{3,7},{4,0},{5,1},{6,2},{7,3},{8,12},{9,13},{10,... | collective-permute-start | bytes 24584 | tf_op jit(solution)/shard_map/ppermute | solution.py:29
  79.4 6.6 %collective-permute-start.4 = (bf16[1,16,16,16]{3,2,1,0:T(8,128)(2,1)S(1)}, bf16[1,16,16,16]{3,2,1,0:T(8,128)(2,1)S(1)}, u32[]{:S(2)}, u32[]{:S(2)}) collective-permute-start(bf16[1,16,16,16]{3,2,1,0:T(8,128)(2,1)S(1)} %get-tuple-element.168), channel_id=1, source_target_pairs={{0,5},{1,4},{2,7},{3,6},{4,1},{5,0},{6,3},{7,2},{8,13},{9,12},{10,... | collective-permute-start | bytes 24584 | tf_op jit(solution)/shard_map/ppermute | solution.py:29
  79.6 9.4 %collective-permute-start.5 = (bf16[1,16,16,16]{3,2,1,0:T(8,128)(2,1)S(1)}, bf16[1,16,16,16]{3,2,1,0:T(8,128)(2,1)S(1)}, u32[]{:S(2)}, u32[]{:S(2)}) collective-permute-start(bf16[1,16,16,16]{3,2,1,0:T(8,128)(2,1)S(1)} %get-tuple-element.167), channel_id=1, source_target_pairs={{0,6},{1,7},{2,4},{3,5},{4,2},{5,3},{6,0},{7,1},{8,14},{9,15},{10,... | collective-permute-start | bytes 24584 | tf_op jit(solution)/shard_map/ppermute | solution.py:29
  82.3 7.1 %collective-permute-start.6 = (bf16[1,16,16,16]{3,2,1,0:T(8,128)(2,1)S(1)}, bf16[1,16,16,16]{3,2,1,0:T(8,128)(2,1)S(1)}, u32[]{:S(2)}, u32[]{:S(2)}) collective-permute-start(bf16[1,16,16,16]{3,2,1,0:T(8,128)(2,1)S(1)} %get-tuple-element.166), channel_id=1, source_target_pairs={{0,7},{1,6},{2,5},{3,4},{4,3},{5,2},{6,1},{7,0},{8,15},{9,14},{10,... | collective-permute-start | bytes 24584 | tf_op jit(solution)/shard_map/ppermute | solution.py:29
  82.4 10.3 %collective-permute-start.7 = (bf16[1,16,16,16]{3,2,1,0:T(8,128)(2,1)S(1)}, bf16[1,16,16,16]{3,2,1,0:T(8,128)(2,1)S(1)}, u32[]{:S(2)}, u32[]{:S(2)}) collective-permute-start(bf16[1,16,16,16]{3,2,1,0:T(8,128)(2,1)S(1)} %get-tuple-element.165), channel_id=1, source_target_pairs={{0,8},{1,9},{2,10},{3,11},{4,12},{5,13},{6,14},{7,15},{8,0},{9,1},... | collective-permute-start | bytes 24584 | tf_op jit(solution)/shard_map/ppermute | solution.py:29
  85.2 11.8 %collective-permute-start.8 = (bf16[1,16,16,16]{3,2,1,0:T(8,128)(2,1)S(1)}, bf16[1,16,16,16]{3,2,1,0:T(8,128)(2,1)S(1)}, u32[]{:S(2)}, u32[]{:S(2)}) collective-permute-start(bf16[1,16,16,16]{3,2,1,0:T(8,128)(2,1)S(1)} %get-tuple-element.164), channel_id=1, source_target_pairs={{0,9},{1,8},{2,11},{3,10},{4,13},{5,12},{6,15},{7,14},{8,1},{9,0},... | collective-permute-start | bytes 24584 | tf_op jit(solution)/shard_map/ppermute | solution.py:29
  86.0 14.9 %collective-permute-start.9 = (bf16[1,16,16,16]{3,2,1,0:T(8,128)(2,1)S(1)}, bf16[1,16,16,16]{3,2,1,0:T(8,128)(2,1)S(1)}, u32[]{:S(2)}, u32[]{:S(2)}) collective-permute-start(bf16[1,16,16,16]{3,2,1,0:T(8,128)(2,1)S(1)} %get-tuple-element.163), channel_id=1, source_target_pairs={{0,10},{1,11},{2,8},{3,9},{4,14},{5,15},{6,12},{7,13},{8,2},{9,3},... | collective-permute-start | bytes 24584 | tf_op jit(solution)/shard_map/ppermute | solution.py:29
  88.9 15.1 %collective-permute-start.10 = (bf16[1,16,16,16]{3,2,1,0:T(8,128)(2,1)S(1)}, bf16[1,16,16,16]{3,2,1,0:T(8,128)(2,1)S(1)}, u32[]{:S(2)}, u32[]{:S(2)}) collective-permute-start(bf16[1,16,16,16]{3,2,1,0:T(8,128)(2,1)S(1)} %get-tuple-element.162), channel_id=1, source_target_pairs={{0,11},{1,10},{2,9},{3,8},{4,15},{5,14},{6,13},{7,12},{8,3},{9,2},... | collective-permute-start | bytes 24584 | tf_op jit(solution)/shard_map/ppermute | solution.py:29
  89.4 14.7 %collective-permute-start.11 = (bf16[1,16,16,16]{3,2,1,0:T(8,128)(2,1)S(1)}, bf16[1,16,16,16]{3,2,1,0:T(8,128)(2,1)S(1)}, u32[]{:S(2)}, u32[]{:S(2)}) collective-permute-start(bf16[1,16,16,16]{3,2,1,0:T(8,128)(2,1)S(1)} %get-tuple-element.161), channel_id=1, source_target_pairs={{0,12},{1,13},{2,14},{3,15},{4,8},{5,9},{6,10},{7,11},{8,4},{9,5},... | collective-permute-start | bytes 24584 | tf_op jit(solution)/shard_map/ppermute | solution.py:29
  92.8 11.4 %collective-permute-start.12 = (bf16[1,16,16,16]{3,2,1,0:T(8,128)(2,1)S(1)}, bf16[1,16,16,16]{3,2,1,0:T(8,128)(2,1)S(1)}, u32[]{:S(2)}, u32[]{:S(2)}) collective-permute-start(bf16[1,16,16,16]{3,2,1,0:T(8,128)(2,1)S(1)} %get-tuple-element.160), channel_id=1, source_target_pairs={{0,13},{1,12},{2,15},{3,14},{4,9},{5,8},{6,11},{7,10},{8,5},{9,4},... | collective-permute-start | bytes 24584 | tf_op jit(solution)/shard_map/ppermute | solution.py:29
  97.0 7.1 %collective-permute-start.13 = (bf16[1,16,16,16]{3,2,1,0:T(8,128)(2,1)S(1)}, bf16[1,16,16,16]{3,2,1,0:T(8,128)(2,1)S(1)}, u32[]{:S(2)}, u32[]{:S(2)}) collective-permute-start(bf16[1,16,16,16]{3,2,1,0:T(8,128)(2,1)S(1)} %get-tuple-element.159), channel_id=1, source_target_pairs={{0,14},{1,15},{2,12},{3,13},{4,10},{5,11},{6,8},{7,9},{8,6},{9,7},... | collective-permute-start | bytes 24584 | tf_op jit(solution)/shard_map/ppermute | solution.py:29
  100.9 6.9 %collective-permute-start.14 = (bf16[1,16,16,16]{3,2,1,0:T(8,128)(2,1)S(1)}, bf16[1,16,16,16]{3,2,1,0:T(8,128)(2,1)S(1)}, u32[]{:S(2)}, u32[]{:S(2)}) collective-permute-start(bf16[1,16,16,16]{3,2,1,0:T(8,128)(2,1)S(1)} %get-tuple-element.158), channel_id=1, source_target_pairs={{0,15},{1,14},{2,13},{3,12},{4,11},{5,10},{6,9},{7,8},{8,7},{9,6},... | collective-permute-start | bytes 24584 | tf_op jit(solution)/shard_map/ppermute | solution.py:29
  110.5 12.0 %collective-permute-start.15 = (bf16[256,15,16]{0,2,1:T(8,128)(2,1)S(1)}, bf16[256,15,16]{0,2,1:T(8,128)(2,1)S(1)}, u32[]{:S(2)}, u32[]{:S(2)}) collective-permute-start(bf16[256,15,16]{0,2,1:T(8,128)(2,1)S(1)} %slice.146), channel_id=1, source_target_pairs={{8,0},{9,1},{10,2},{11,3},{12,4},{13,5},{14,6},{15,7},{24,16},{25,... | collective-permute-start | bytes 368648 | tf_op jit(solution)/shard_map/ppermute | solution.py:37
